TPU v7x, 32 devices: a whole 2x2x4 slice. The times are simulated.
32 devices in a mesh: dp: 16 (over z, y, x), mp: 2 (over core).
Axes of the slice: x: 2, y: 2, z: 4, core: 2. Of those that a mesh axis runs over, the one named last changes fastest.
Arguments:
- variates: bfloat16 [45568, 512], P(('dp', 'mp')), may hold values from -6 to 6
- dataset: int32 [32], P('dp'), may hold values from 0 to 3
- w_qkv: bfloat16 [3, 512, 512], P(None, None, 'mp'), may hold values from -0.25 to 0.25
- b_qv: bfloat16 [2, 512], P(None, 'mp'), may hold values from -3 to 3
- w_out: bfloat16 [512, 512], P('mp'), may hold values from -0.75 to 0.75
- b_out: bfloat16 [512], replicated, may hold values from -2 to 2
- gain_one: bfloat16 [512], replicated, may hold values from 0.5 to 1.5
- shift_one: bfloat16 [512], replicated, may hold values from -2 to 2
- w_up: bfloat16 [512, 2048], P(None, 'mp'), may hold values from -0.25 to 0.25
- b_up: bfloat16 [2048], P('mp'), may hold values from -3 to 3
- w_down: bfloat16 [2048, 512], P('mp'), may hold values from -0.1875 to 0.1875
- b_down: bfloat16 [512], replicated, may hold values from -2 to 2
- gain_two: bfloat16 [512], replicated, may hold values from 0.5 to 1.5
- shift_two: bfloat16 [512], replicated, may hold values from -2 to 2
- cotangent: bfloat16 [45568, 512], P(('dp', 'mp')), may hold values from -6 to 6
Outputs:
- output: bfloat16 [45568, 512], P(('dp', 'mp'))
- grad_input: float32 [45568, 512], P(('dp', 'mp'))
- grad_w_qkv: float32 [3, 512, 512], P(None, None, 'mp')
- grad_b_qv: float32 [2, 512], P(None, 'mp')
- grad_w_out: float32 [512, 512], P('mp')
- grad_b_out: float32 [512], replicated
- grad_gain_one: float32 [512], replicated
- grad_shift_one: float32 [512], replicated
- grad_w_up: float32 [512, 2048], P(None, 'mp')
- grad_b_up: float32 [2048], P('mp')
- grad_w_down: float32 [2048, 512], P('mp')
- grad_b_down: float32 [512], replicated
- grad_gain_two: float32 [512], replicated
- grad_shift_two: float32 [512], replicated
Inputs may be any that keep to these rules, and one draw needn't show every extreme that they name: dataset numbers 0, 1, 2, 3 stand for windows of 7, 21, 321 and 862 variates.
All inputs are finite; a program needn't handle non-finite values.
Results may differ from a plain program's by a relative error of at most 0.012.
Values may be sent and summed in bfloat16 or wider, within the bound.
No kernel may reach another device: no remote copies, remote signals or barrier semaphores. Data moves between devices by JAX's collectives and lax.ppermute only.
A program may use at most 256 MiB of HBM per device.

v0:
```python
import jax
import jax.numpy as jnp
from jax import lax
from jax.sharding import PartitionSpec as P

HEAD_DIM = 64
SLOTS = 1424
WIN_ETT = 7
WIN_WEATHER = 21
WIN_ELEC = 321
WIN_TRAFFIC = 862


epsilon = 1e-05


def window_layout(dataset):
    widths = jnp.array([WIN_ETT, WIN_WEATHER, WIN_ELEC, WIN_TRAFFIC], jnp.int32)
    chosen = (dataset[:, None] == jnp.arange(4, dtype=jnp.int32)[None, :]).astype(jnp.int32)
    window = jnp.sum(chosen * widths[None, :], axis=1)
    places = jnp.arange(SLOTS, dtype=jnp.int32)[None, :]
    filled = SLOTS // window * window
    occupied = places < filled[:, None]
    segment = jnp.where(occupied, places // window[:, None], -1)
    return (segment, occupied)


def normalize(matrix, gain_vec, shift_vec):
    centre = matrix - jnp.mean(matrix, axis=1, keepdims=True)
    spread = lax.rsqrt(jnp.mean(centre * centre, axis=1, keepdims=True) + epsilon)
    normed = centre * spread
    return (normed * gain_vec.astype(jnp.float32) + shift_vec.astype(jnp.float32), normed, spread)


def norm_back(grad_rows, normed, spread, gain_vec):
    scaled = grad_rows * gain_vec.astype(jnp.float32)
    return spread * (
        scaled
        - jnp.mean(scaled, axis=1, keepdims=True)
        - normed * jnp.mean(scaled * normed, axis=1, keepdims=True)
    )


def masked_scores(queries, key_rows, segment):
    scores = jnp.einsum(
        "qhd,khd->hqk", queries, key_rows, preferred_element_type=jnp.float32
    ) * HEAD_DIM ** (-0.5)
    allowed = (segment[:, None] == segment[None, :])[None, :, :]
    return jnp.where(allowed, scores, -jnp.inf)


def attend_forward(pieces):
    queries, key_rows, values, segment = pieces
    scores = masked_scores(queries, key_rows, segment)
    maxima = jnp.max(scores, axis=2, keepdims=True)
    raised = jnp.exp(scores - maxima)
    totals = jnp.sum(raised, axis=2, keepdims=True)
    probs = (raised / totals).astype(jnp.bfloat16)
    mixed = jnp.einsum("hqk,khd->qhd", probs, values, preferred_element_type=jnp.float32)
    return (mixed.astype(jnp.bfloat16), maxima[:, :, 0] + jnp.log(totals[:, :, 0]))


def attend_backward(pieces):
    queries, key_rows, values, segment, grad_mixed, logsum = pieces
    scores = masked_scores(queries, key_rows, segment)
    probs = jnp.exp(scores - logsum[:, :, None])
    grad_probs = jnp.einsum("qhd,khd->hqk", grad_mixed, values, preferred_element_type=jnp.float32)
    grad_scores = (
        probs * (grad_probs - jnp.sum(probs * grad_probs, axis=2, keepdims=True))
    ).astype(jnp.bfloat16)
    scaling = HEAD_DIM ** (-0.5)
    grad_q = (
        jnp.einsum("hqk,khd->qhd", grad_scores, key_rows, preferred_element_type=jnp.float32)
        * scaling
    ).astype(jnp.bfloat16)
    grad_k = (
        jnp.einsum("hqk,qhd->khd", grad_scores, queries, preferred_element_type=jnp.float32)
        * scaling
    ).astype(jnp.bfloat16)
    grad_v = jnp.einsum(
        "hqk,qhd->khd", probs.astype(jnp.bfloat16), grad_mixed, preferred_element_type=jnp.float32
    ).astype(jnp.bfloat16)
    return (grad_q, grad_k, grad_v)


def gelu_slope(pre_act):
    density = jnp.exp(-0.5 * pre_act * pre_act) * (2.0 * jnp.pi) ** (-0.5)
    return 0.5 * (1.0 + lax.erf(pre_act * 2.0 ** (-0.5))) + pre_act * density


def per_device(
    variates,
    dataset,
    w_qkv,
    b_qv,
    w_out,
    b_out,
    gain_one,
    shift_one,
    w_up,
    b_up,
    w_down,
    b_down,
    gain_two,
    shift_two,
    cotangent,
):
    shard_rows = variates.shape[0]
    segment, occupied = window_layout(dataset)
    row_start = lax.axis_index("mp") * shard_rows
    used_rows = lax.dynamic_slice_in_dim(
        occupied.reshape(-1).astype(jnp.float32), row_start, shard_rows, 0
    )
    source = lax.all_gather(variates, "mp", axis=0, tiled=True)
    qkv_weight, qv_bias, out_weight = (w_qkv, b_qv, w_out)
    attn_width = out_weight.shape[0]
    attn_heads = attn_width // HEAD_DIM
    projected = jnp.einsum("rd,jde->jre", source, qkv_weight, preferred_element_type=jnp.float32)
    queries = (projected[0] + qv_bias[0].astype(jnp.float32)).astype(jnp.bfloat16)
    key_rows = projected[1].astype(jnp.bfloat16)
    values = (projected[2] + qv_bias[1].astype(jnp.float32)).astype(jnp.bfloat16)
    head_shape = (segment.shape[0], SLOTS, attn_heads, HEAD_DIM)
    query_heads = queries.reshape(head_shape)
    key_heads = key_rows.reshape(head_shape)
    value_heads = values.reshape(head_shape)
    mixed, logsum = lax.map(attend_forward, (query_heads, key_heads, value_heads, segment))
    mixed = mixed.reshape(-1, attn_width)
    attn_part = jnp.dot(mixed, out_weight, preferred_element_type=jnp.float32)
    attn_sum = lax.psum_scatter(attn_part, "mp", scatter_dimension=0, tiled=True)
    resid_one = variates.astype(jnp.float32) + attn_sum + b_out.astype(jnp.float32)
    hidden_one, normed_one, spread_one = normalize(resid_one, gain_one, shift_one)
    mid_low = hidden_one.astype(jnp.bfloat16)
    mid_whole = lax.all_gather(mid_low, "mp", axis=0, tiled=True)
    pre_act = jnp.dot(mid_whole, w_up, preferred_element_type=jnp.float32) + b_up.astype(
        jnp.float32
    )
    activated = jax.nn.gelu(pre_act, approximate=False).astype(jnp.bfloat16)
    ffn_out = lax.psum_scatter(
        jnp.dot(activated, w_down, preferred_element_type=jnp.float32),
        "mp",
        scatter_dimension=0,
        tiled=True,
    )
    second = hidden_one + ffn_out + b_down.astype(jnp.float32)
    result, normed_two, spread_two = normalize(second, gain_two, shift_two)
    grad_top = cotangent.astype(jnp.float32) * used_rows[:, None]
    grad_gain_two = jnp.sum(grad_top * normed_two, axis=0)
    grad_shift_two = jnp.sum(grad_top, axis=0)
    grad_second = norm_back(grad_top, normed_two, spread_two, gain_two)
    grad_b_down = jnp.sum(grad_second, axis=0)
    grad_ffn = grad_second.astype(jnp.bfloat16)
    grad_ffn_whole = lax.all_gather(grad_ffn, "mp", axis=0, tiled=True)
    grad_w_down = jnp.einsum(
        "rf,rd->fd", activated, grad_ffn_whole, preferred_element_type=jnp.float32
    )
    grad_inner = jnp.einsum("rd,fd->rf", grad_ffn_whole, w_down, preferred_element_type=jnp.float32)
    grad_pre = (grad_inner * gelu_slope(pre_act)).astype(jnp.bfloat16)
    grad_w_up = jnp.einsum("rd,rf->df", mid_whole, grad_pre, preferred_element_type=jnp.float32)
    grad_b_up = jnp.sum(grad_pre.astype(jnp.float32), axis=0)
    mid_part = jnp.einsum("rf,df->rd", grad_pre, w_up, preferred_element_type=jnp.float32)
    grad_mid = lax.psum_scatter(mid_part, "mp", scatter_dimension=0, tiled=True)
    grad_hidden = grad_second + grad_mid
    grad_gain_one = jnp.sum(grad_hidden * normed_one, axis=0)
    grad_shift_one = jnp.sum(grad_hidden, axis=0)
    grad_resid = norm_back(grad_hidden, normed_one, spread_one, gain_one)
    grad_b_out = jnp.sum(grad_resid, axis=0)
    grad_mix_out = grad_resid.astype(jnp.bfloat16)
    grad_mix_whole = lax.all_gather(grad_mix_out, "mp", axis=0, tiled=True)
    grad_w_out = jnp.einsum("rc,rd->cd", mixed, grad_mix_whole, preferred_element_type=jnp.float32)
    grad_mixed = jnp.einsum(
        "rd,cd->rc", grad_mix_whole, out_weight, preferred_element_type=jnp.float32
    ).astype(jnp.bfloat16)
    grad_q, grad_k, grad_v = lax.map(
        attend_backward,
        (query_heads, key_heads, value_heads, segment, grad_mixed.reshape(head_shape), logsum),
    )
    grad_proj = jnp.stack(
        [
            grad_q.reshape(-1, attn_width),
            grad_k.reshape(-1, attn_width),
            grad_v.reshape(-1, attn_width),
        ]
    )
    grad_w_qkv = jnp.einsum("rd,jre->jde", source, grad_proj, preferred_element_type=jnp.float32)
    grad_b_qv = jnp.stack(
        [
            jnp.sum(grad_proj[0].astype(jnp.float32), axis=0),
            jnp.sum(grad_proj[2].astype(jnp.float32), axis=0),
        ]
    )
    input_part = jnp.einsum(
        "jre,jde->rd", grad_proj, qkv_weight, preferred_element_type=jnp.float32
    )
    grad_input = grad_resid + lax.psum_scatter(
        input_part.astype(jnp.bfloat16), "mp", scatter_dimension=0, tiled=True
    ).astype(jnp.float32)
    total_qkv, total_bqv, total_out = lax.psum((grad_w_qkv, grad_b_qv, grad_w_out), "dp")
    total_w_up, total_b_up, total_w_down = lax.psum((grad_w_up, grad_b_up, grad_w_down), "dp")
    common = lax.psum(
        (grad_b_out, grad_gain_one, grad_shift_one, grad_b_down, grad_gain_two, grad_shift_two),
        ("dp", "mp"),
    )
    return (
        result.astype(jnp.bfloat16),
        grad_input,
        total_qkv,
        total_bqv,
        total_out,
        common[0],
        common[1],
        common[2],
        total_w_up,
        total_b_up,
        total_w_down,
        common[3],
        common[4],
        common[5],
    )


def solution(mesh):
    placed = (
        P(("dp", "mp"), None),
        P("dp"),
        P(None, None, "mp"),
        P(None, "mp"),
        P("mp", None),
        P(),
        P(),
        P(),
        P(None, "mp"),
        P("mp"),
        P("mp", None),
        P(),
        P(),
        P(),
        P(("dp", "mp"), None),
    )
    return jax.shard_map(
        per_device,
        mesh=mesh,
        in_specs=placed,
        out_specs=(
            P(("dp", "mp"), None),
            P(("dp", "mp"), None),
            P(None, None, "mp"),
            P(None, "mp"),
            P("mp", None),
            P(),
            P(),
            P(),
            P(None, "mp"),
            P("mp"),
            P("mp", None),
            P(),
            P(),
            P(),
        ),
        check_vma=False,
    )
```

profile of v0, /device:TPU:0, one launch (start us, length us, event | category | flops | bytes accessed | tf_op | source)
XLA Modules:
  0.0 892.3 jit_solution(6141213658963963988)
XLA Ops:
  10.5 13.6 %all-gather.5.cloned.1.call-done = bf16[2848,512]{1,0:T(8,128)(2,1)} async-done(((bf16[1424,512]{1,0:T(8,128)(2,1)}), bf16[2848,512]{1,0:T(8,128)(2,1)}) %all-gather.5.cloned.1.call-update) | async-done | bytes 2916368 | tf_op jit(solution)/shard_map/all_gather | solution.py:114
  72.0 91.9 %while.26 = (s32[]{:T(128)}, bf16[2,1424,4,64]{1,3,2,0:T(8,128)(2,1)}, f32[2,4,1424]{2,1,0:T(4,128)S(1)}, bf16[2,1424,4,64]{1,3,2,0:T(8,128)(2,1)}, s32[2,1424]{...) while((s32[]{:T(128)}, ...), condition=%wide.region_4.5_spmd, body=%wide.region_1.4_spmd.sunk | while | flops 2143718144 | bytes 122402680 | solution.py:126
  73.9 14.8 %fusion.138 = (f32[4,1424]{1,0:T(4,128)S(1)}, f32[4,1424,1424]{1,2,0:T(8,128)}) fusion(bf16[2,1424,4,64]{1,3,2,0:T(8,128)(2,1)} %get-tuple-element.418, s32[]{:T(128)S(6)} %copy.111, bf16[2,1424,4,64]{1,3,2,0:T(8,128)(2,1)S(1)} %get-tuple-element.417, pred[1424,1424]{0,1:T(8,128)(4,1)S(1)} %broadcast_compare_fusion.4), kind=kOutput, calls=%fused_computation.149.clone.1 | convolution fusion | flops 1062548928 | bytes 36228352 | tf_op jit(solution)/shard_map/while/body/eval_jaxpr/qhd,khd->hqk/dot_general | solution.py:45
  88.7 14.1 %fusion.139 = f32[4,1424]{1,0:T(4,128)S(1)} fusion(f32[4,1424,1424]{1,2,0:T(8,128)} %get-tuple-element.382, f32[4,1424]{1,0:T(4,128)S(1)} %get-tuple-element.383), kind=kLoop, calls=%fused_computation.4.clone.1 | loop fusion | flops 16216512 | bytes 32489984 | tf_op jit(solution)/shard_map/while/body/eval_jaxpr/reduce_sum | solution.py:57
  102.8 14.1 %fusion.140 = bf16[2,1424,4,64]{1,3,2,0:T(8,128)(2,1)S(1)} fusion(bf16[2,1424,4,64]{1,3,2,0:T(8,128)(2,1)S(1)} %copy-done.10, s32[]{:T(128)S(6)} %copy.111, f32[4,1424,1424]{1,2,0:T(8,128)} %get-tuple-element.382, f32[4,1424]{1,0:T(4,128)S(1)} %fusion.139, f32[4,1424]{1,0:T(4,128)S(1)} %get-tuple-element.383, bf16[2,1424,4,64]{1,3,2,0:T(8,128)(2,1)S(1)} %copy-done.7), kind=kOutput, calls=%fused_computation.9.clone.1 | convolution fusion | flops 1062919168 | bytes 34067456 | tf_op jit(solution)/shard_map/while/body/eval_jaxpr/hqk,khd->qhd/dot_general | solution.py:59
  119.7 14.8 %fusion.138 = (f32[4,1424]{1,0:T(4,128)S(1)}, f32[4,1424,1424]{1,2,0:T(8,128)}) fusion(bf16[2,1424,4,64]{1,3,2,0:T(8,128)(2,1)} %get-tuple-element.418, s32[]{:T(128)S(6)} %copy.111, bf16[2,1424,4,64]{1,3,2,0:T(8,128)(2,1)S(1)} %get-tuple-element.417, pred[1424,1424]{0,1:T(8,128)(4,1)S(1)} %broadcast_compare_fusion.4), kind=kOutput, calls=%fused_computation.149.clone.1 | convolution fusion | flops 1062548928 | bytes 36228352 | tf_op jit(solution)/shard_map/while/body/eval_jaxpr/qhd,khd->hqk/dot_general | solution.py:45
  134.5 14.1 %fusion.139 = f32[4,1424]{1,0:T(4,128)S(1)} fusion(f32[4,1424,1424]{1,2,0:T(8,128)} %get-tuple-element.382, f32[4,1424]{1,0:T(4,128)S(1)} %get-tuple-element.383), kind=kLoop, calls=%fused_computation.4.clone.1 | loop fusion | flops 16216512 | bytes 32489984 | tf_op jit(solution)/shard_map/while/body/eval_jaxpr/reduce_sum | solution.py:57
  148.6 14.1 %fusion.140 = bf16[2,1424,4,64]{1,3,2,0:T(8,128)(2,1)S(1)} fusion(bf16[2,1424,4,64]{1,3,2,0:T(8,128)(2,1)S(1)} %copy-done.10, s32[]{:T(128)S(6)} %copy.111, f32[4,1424,1424]{1,2,0:T(8,128)} %get-tuple-element.382, f32[4,1424]{1,0:T(4,128)S(1)} %fusion.139, f32[4,1424]{1,0:T(4,128)S(1)} %get-tuple-element.383, bf16[2,1424,4,64]{1,3,2,0:T(8,128)(2,1)S(1)} %copy-done.7), kind=kOutput, calls=%fused_computation.9.clone.1 | convolution fusion | flops 1062919168 | bytes 34067456 | tf_op jit(solution)/shard_map/while/body/eval_jaxpr/hqk,khd->qhd/dot_general | solution.py:59
  178.6 14.5 %reduce-scatter.5.cloned.1.call-done = f32[1424,512]{1,0:T(8,128)} async-done(((f32[2848,512]{1,0:T(8,128)}), f32[1424,512]{1,0:T(8,128)}) %reduce-scatter.5.cloned.1.call-update) | async-done | bytes 2916368 | tf_op jit(solution)/shard_map/reduce_scatter | solution.py:129
  199.1 13.1 %all-gather.7.cloned.1.call-done = bf16[2848,512]{1,0:T(8,128)(2,1)} async-done(((bf16[1424,512]{1,0:T(8,128)(2,1)}), bf16[2848,512]{1,0:T(8,128)(2,1)}) %all-gather.7.cloned.1.call-update) | async-done | bytes 2916368 | tf_op jit(solution)/shard_map/all_gather | solution.py:133
  212.3 29.7 %fusion.56 = (bf16[2848,1024]{1,0:T(8,128)(2,1)S(1)}, f32[2848,1024]{1,0:T(8,128)}) fusion(f32[1024]{0:T(1024)S(1)} %convert_element_type.132, bf16[2848,512]{1,0:T(8,128)(2,1)} %all-gather.7.cloned.1.call-done, bf16[512,1024]{1,0:T(8,128)(2,1)S(1)} %copy-done), kind=kOutput, calls=%fused_computation.66 | convolution fusion | flops 3178823680 | bytes 21467136 | tf_op jit(solution)/shard_map/dot_general | solution.py:134
  250.4 14.3 %reduce-scatter.7.cloned.1.call-done = f32[1424,512]{1,0:T(8,128)} async-done(((f32[2848,512]{1,0:T(8,128)}), f32[1424,512]{1,0:T(8,128)}) %reduce-scatter.7.cloned.1.call-update) | async-done | bytes 2916368 | tf_op jit(solution)/shard_map/reduce_scatter | solution.py:138
  278.4 13.1 %all-gather.9.cloned.1.call-done = bf16[2848,512]{1,0:T(8,128)(2,1)} async-done(((bf16[1424,512]{1,0:T(8,128)(2,1)}), bf16[2848,512]{1,0:T(8,128)(2,1)}) %all-gather.9.cloned.1.call-update) | async-done | bytes 2916368 | tf_op jit(solution)/shard_map/all_gather | solution.py:152
  291.5 10.3 %convert_reduce_fusion = (f32[1024]{0:T(1024)}, bf16[2848,1024]{1,0:T(8,128)(2,1)S(1)}) fusion(f32[2848,1024]{1,0:T(8,128)} %get-tuple-element.279, f32[1024]{0:T(1024)S(1)} %convert_element_type.132, bf16[2848,512]{1,0:T(8,128)(2,1)} %all-gather.9.cloned.1.call-done, bf16[1024,512]{1,0:T(8,128)(2,1)} %param.30), kind=kOutput, calls=%fused_computation.73 | convolution fusion | flops 3024256000 | bytes 21471232 | tf_op jit(solution)/shard_map/rd,fd->rf/dot_general | solution.py:156
  310.0 15.2 %reduce-scatter.9.cloned.1.call-done = f32[1424,512]{1,0:T(8,128)} async-done(((f32[2848,512]{1,0:T(8,128)}), f32[1424,512]{1,0:T(8,128)}) %reduce-scatter.9.cloned.1.call-update) | async-done | bytes 2916368 | tf_op jit(solution)/shard_map/reduce_scatter | solution.py:161
  336.4 13.1 %all-gather.11.cloned.1.call-done = bf16[2848,512]{1,0:T(8,128)(2,1)} async-done(((bf16[1424,512]{1,0:T(8,128)(2,1)}), bf16[2848,512]{1,0:T(8,128)(2,1)}) %all-gather.11.cloned.1.call-update) | async-done | bytes 2916368 | tf_op jit(solution)/shard_map/all_gather | solution.py:168
  368.0 233.6 %while.27 = (s32[]{:T(128)}, bf16[2,1424,4,64]{1,3,2,0:T(8,128)(2,1)}, bf16[2,1424,4,64]{1,3,2,0:T(8,128)(2,1)}, bf16[2,1424,4,64]{1,3,2,0:T(8,128)(2,1)}, bf16[...) while((s32[]{:T(128)}, ...), condition=%wide.region_18.19_spmd, body=%wide.region_16.18_spmd.sunk | while | flops 5267951616 | bytes 274710144 | solution.py:173
  371.1 17.6 %fusion.149 = f32[4,1424,1424]{1,2,0:T(8,128)} fusion(bf16[2,1424,4,64]{1,3,2,0:T(8,128)(2,1)} %get-tuple-element.451, s32[]{:T(128)S(6)} %copy.121, bf16[2,1424,4,64]{1,3,2,0:T(8,128)(2,1)} %get-tuple-element.450), kind=kOutput, calls=%fused_computation.40.clone.1 | convolution fusion | flops 1038221312 | bytes 34018304 | tf_op jit(solution)/shard_map/while/body/eval_jaxpr/qhd,khd->hqk/dot_general | solution.py:67
  388.7 29.7 %multiply_reduce_fusion.9 = (f32[4,1424]{1,0:T(4,128)S(1)}, f32[4,1424,1424]{1,2,0:T(8,128)}) fusion(f32[4,1424,1424]{1,2,0:T(8,128)} %fusion.149, f32[4,1424]{1,0:T(4,128)S(1)} %dynamic-slice_bitcast_fusion.2, bf16[2,1424,4,64]{1,3,2,0:T(8,128)(2,1)} %get-tuple-element.446, s32[]{:T(128)S(6)} %copy.121, bf16[2,1424,4,64]{1,3,2,0:T(8,128)(2,1)} %copy-done.3, ...), kind=kOutput, calls=%fused_computation.24.clone.1 | convolution fusion | flops 1078771200 | bytes 71087872 | tf_op jit(solution)/shard_map/while/body/eval_jaxpr/qhd,khd->hqk/dot_general | solution.py:45
  418.4 29.5 %multiply_convert_fusion.2 = bf16[4,1424,1424]{1,2,0:T(8,128)(2,1)} fusion(f32[4,1424,1424]{1,2,0:T(8,128)} %get-tuple-element.394, f32[4,1424,1424]{1,2,0:T(8,128)} %fusion.149, f32[4,1424]{1,0:T(4,128)S(1)} %get-tuple-element.395), kind=kLoop, calls=%fused_computation.23.clone.1 | loop fusion | flops 24333312 | bytes 81133824 | tf_op jit(solution)/shard_map/while/body/eval_jaxpr/convert_element_type | solution.py:70
  447.9 14.9 %fusion.152 = bf16[2,1424,4,64]{1,3,2,0:T(8,128)(2,1)} fusion(bf16[2,1424,4,64]{1,3,2,0:T(8,128)(2,1)} %get-tuple-element.434, s32[]{:T(128)S(6)} %copy.121, f32[4,1424,1424]{1,2,0:T(8,128)} %get-tuple-element.394, bf16[2,1424,4,64]{1,3,2,0:T(8,128)(2,1)} %get-tuple-element.450), kind=kOutput, calls=%fused_computation.39.clone.1 | convolution fusion | flops 1046696960 | bytes 36570112 | tf_op jit(solution)/shard_map/while/body/eval_jaxpr/hqk,qhd->khd/dot_general | solution.py:80
  462.8 11.9 %fusion.151 = bf16[2,1424,4,64]{1,3,2,0:T(8,128)(2,1)} fusion(bf16[2,1424,4,64]{1,3,2,0:T(8,128)(2,1)} %get-tuple-element.433, s32[]{:T(128)S(6)} %copy.121, bf16[4,1424,1424]{1,2,0:T(8,128)(2,1)} %multiply_convert_fusion.2, bf16[2,1424,4,64]{1,3,2,0:T(8,128)(2,1)S(1)} %copy-done.4), kind=kOutput, calls=%fused_computation.35.clone.1 | convolution fusion | flops 1038950400 | bytes 19072000 | tf_op jit(solution)/shard_map/while/body/eval_jaxpr/hqk,qhd->khd/dot_general | solution.py:77
  474.7 10.3 %fusion.150 = bf16[2,1424,4,64]{1,3,2,0:T(8,128)(2,1)} fusion(bf16[2,1424,4,64]{1,3,2,0:T(8,128)(2,1)} %get-tuple-element.432, s32[]{:T(128)S(6)} %copy.121, bf16[4,1424,1424]{1,2,0:T(8,128)(2,1)} %multiply_convert_fusion.2, bf16[2,1424,4,64]{1,3,2,0:T(8,128)(2,1)} %get-tuple-element.446), kind=kOutput, calls=%fused_computation.37.clone.1 | convolution fusion | flops 1038950400 | bytes 19072000 | tf_op jit(solution)/shard_map/while/body/eval_jaxpr/hqk,khd->qhd/dot_general | solution.py:73
  487.6 17.6 %fusion.149 = f32[4,1424,1424]{1,2,0:T(8,128)} fusion(bf16[2,1424,4,64]{1,3,2,0:T(8,128)(2,1)} %get-tuple-element.451, s32[]{:T(128)S(6)} %copy.121, bf16[2,1424,4,64]{1,3,2,0:T(8,128)(2,1)} %get-tuple-element.450), kind=kOutput, calls=%fused_computation.40.clone.1 | convolution fusion | flops 1038221312 | bytes 34018304 | tf_op jit(solution)/shard_map/while/body/eval_jaxpr/qhd,khd->hqk/dot_general | solution.py:67
  505.2 29.7 %multiply_reduce_fusion.9 = (f32[4,1424]{1,0:T(4,128)S(1)}, f32[4,1424,1424]{1,2,0:T(8,128)}) fusion(f32[4,1424,1424]{1,2,0:T(8,128)} %fusion.149, f32[4,1424]{1,0:T(4,128)S(1)} %dynamic-slice_bitcast_fusion.2, bf16[2,1424,4,64]{1,3,2,0:T(8,128)(2,1)} %get-tuple-element.446, s32[]{:T(128)S(6)} %copy.121, bf16[2,1424,4,64]{1,3,2,0:T(8,128)(2,1)} %copy-done.3, ...), kind=kOutput, calls=%fused_computation.24.clone.1 | convolution fusion | flops 1078771200 | bytes 71087872 | tf_op jit(solution)/shard_map/while/body/eval_jaxpr/qhd,khd->hqk/dot_general | solution.py:45
  534.9 29.5 %multiply_convert_fusion.2 = bf16[4,1424,1424]{1,2,0:T(8,128)(2,1)} fusion(f32[4,1424,1424]{1,2,0:T(8,128)} %get-tuple-element.394, f32[4,1424,1424]{1,2,0:T(8,128)} %fusion.149, f32[4,1424]{1,0:T(4,128)S(1)} %get-tuple-element.395), kind=kLoop, calls=%fused_computation.23.clone.1 | loop fusion | flops 24333312 | bytes 81133824 | tf_op jit(solution)/shard_map/while/body/eval_jaxpr/convert_element_type | solution.py:70
  564.4 14.9 %fusion.152 = bf16[2,1424,4,64]{1,3,2,0:T(8,128)(2,1)} fusion(bf16[2,1424,4,64]{1,3,2,0:T(8,128)(2,1)} %get-tuple-element.434, s32[]{:T(128)S(6)} %copy.121, f32[4,1424,1424]{1,2,0:T(8,128)} %get-tuple-element.394, bf16[2,1424,4,64]{1,3,2,0:T(8,128)(2,1)} %get-tuple-element.450), kind=kOutput, calls=%fused_computation.39.clone.1 | convolution fusion | flops 1046696960 | bytes 36570112 | tf_op jit(solution)/shard_map/while/body/eval_jaxpr/hqk,qhd->khd/dot_general | solution.py:80
  579.3 11.9 %fusion.151 = bf16[2,1424,4,64]{1,3,2,0:T(8,128)(2,1)} fusion(bf16[2,1424,4,64]{1,3,2,0:T(8,128)(2,1)} %get-tuple-element.433, s32[]{:T(128)S(6)} %copy.121, bf16[4,1424,1424]{1,2,0:T(8,128)(2,1)} %multiply_convert_fusion.2, bf16[2,1424,4,64]{1,3,2,0:T(8,128)(2,1)S(1)} %copy-done.4), kind=kOutput, calls=%fused_computation.35.clone.1 | convolution fusion | flops 1038950400 | bytes 19072000 | tf_op jit(solution)/shard_map/while/body/eval_jaxpr/hqk,qhd->khd/dot_general | solution.py:77
  591.2 10.3 %fusion.150 = bf16[2,1424,4,64]{1,3,2,0:T(8,128)(2,1)} fusion(bf16[2,1424,4,64]{1,3,2,0:T(8,128)(2,1)} %get-tuple-element.432, s32[]{:T(128)S(6)} %copy.121, bf16[4,1424,1424]{1,2,0:T(8,128)(2,1)} %multiply_convert_fusion.2, bf16[2,1424,4,64]{1,3,2,0:T(8,128)(2,1)} %get-tuple-element.446), kind=kOutput, calls=%fused_computation.37.clone.1 | convolution fusion | flops 1038950400 | bytes 19072000 | tf_op jit(solution)/shard_map/while/body/eval_jaxpr/hqk,khd->qhd/dot_general | solution.py:73
  663.6 44.4 %all-reduce = (f32[512]{0:T(512)}, f32[512]{0:T(512)}, f32[512]{0:T(512)}, f32[512]{0:T(512)}, f32[512]{0:T(512)}, /*index=5*/f32[512]{0:T(512)}) all-reduce(f32[512]{0:T(512)S(1)} %copy-done.25, f32[512]{0:T(512)S(1)} %copy-done.22, f32[512]{0:T(512)S(1)} %copy-done.23, ...), channel_id=1, replica_groups=mesh['dp'=16,'mp'=2] {'dp','mp'}, use_global_device_ids=true, to_apply=%region_26.27 | all-reduce | flops 3072 | bytes 24576 | tf_op jit(solution)/shard_map/psum | solution.py:199
  710.2 42.8 %all-reduce.1 = (f32[2,256]{1,0:T(2,128)}, f32[1024]{0:T(1024)}) all-reduce(f32[2,256]{1,0:T(2,128)S(1)} %pad_maximum_fusion, f32[1024]{0:T(1024)S(1)} %copy-done.26), channel_id=1, replica_groups=mesh['dp'=16,'mp'=2] {'dp'}, use_global_device_ids=true, to_apply=%region_23.24 | all-reduce | flops 1536 | bytes 12288 | tf_op jit(solution)/shard_map/psum | solution.py:197
  757.3 121.7 %all-reduce.5.cloned.1.call-done = (f32[3,512,256]{1,2,0:T(8,128)}, f32[256,512]{1,0:T(8,128)}, f32[512,1024]{1,0:T(8,128)}, f32[1024,512]{1,0:T(8,128)}) async-done(((f32[3,512,256]{1,2,0:T(8,128)}, f32[256,512]{1,0:T(8,128)}, f32[512,1024]{1,0:T(8,128)}, f32[1024,512]{1,0:T(8,128)}), (f32[3,512,256]{1,2,0:T(8,128)}, f32[256,512]{1,0:T(8,128)}, f32[512,1024]{1,0:T(8,128)}, ...) | async-done | bytes 6291472 | tf_op jit(solution)/shard_map/psum | solution.py:197
  (217 shorter events, 217.3 us)
Async XLA Ops:
  7.2 205.1 %copy-start = (bf16[512,1024]{1,0:T(8,128)(2,1)S(1)}, bf16[512,1024]{1,0:T(8,128)(2,1)}, u32[]{:S(2)}) copy-start(bf16[512,1024]{1,0:T(8,128)(2,1)} %param.28) | copy-start | bytes 3145732
  7.2 16.9 %all-gather.5.cloned.1.call-start = ((), (), s32[]{:S(2)}) async-start(), calls=%async_computation.4 | async-start | bytes 4374528 | tf_op jit(solution)/shard_map/all_gather | solution.py:114
  7.9 185.2 %reduce-scatter.5.cloned.1.call-start = ((), (), s32[]{:S(2)}) async-start(), calls=%async_computation.5 | async-start | bytes 8749056 | tf_op jit(solution)/shard_map/reduce_scatter | solution.py:129
  9.9 18.6 %copy-start.28 = (s32[2]{0:T(128)}, s32[2]{0:T(128)S(1)}, u32[]{:S(2)}) copy-start(s32[2]{0:T(128)S(1)} %get-tuple-element.277) | copy-start | bytes 28
  88.7 14.1 %copy-start.7 = (bf16[2,1424,4,64]{1,3,2,0:T(8,128)(2,1)S(1)}, bf16[2,1424,4,64]{1,3,2,0:T(8,128)(2,1)}, u32[]{:S(2)}) copy-start(bf16[2,1424,4,64]{1,3,2,0:T(8,128)(2,1)} %get-tuple-element.415) | copy-start | bytes 4374532 | tf_op jit(solution)/shard_map/while
  88.7 14.1 %copy-start.10 = (bf16[2,1424,4,64]{1,3,2,0:T(8,128)(2,1)S(1)}, bf16[2,1424,4,64]{1,3,2,0:T(8,128)(2,1)}, u32[]{:S(2)}) copy-start(bf16[2,1424,4,64]{1,3,2,0:T(8,128)(2,1)} %get-tuple-element.405) | copy-start | bytes 4374532 | tf_op jit(solution)/shard_map/while
  134.4 14.1 %copy-start.7 = (bf16[2,1424,4,64]{1,3,2,0:T(8,128)(2,1)S(1)}, bf16[2,1424,4,64]{1,3,2,0:T(8,128)(2,1)}, u32[]{:S(2)}) copy-start(bf16[2,1424,4,64]{1,3,2,0:T(8,128)(2,1)} %get-tuple-element.415) | copy-start | bytes 4374532 | tf_op jit(solution)/shard_map/while
  134.4 14.1 %copy-start.10 = (bf16[2,1424,4,64]{1,3,2,0:T(8,128)(2,1)S(1)}, bf16[2,1424,4,64]{1,3,2,0:T(8,128)(2,1)}, u32[]{:S(2)}) copy-start(bf16[2,1424,4,64]{1,3,2,0:T(8,128)(2,1)} %get-tuple-element.405) | copy-start | bytes 4374532 | tf_op jit(solution)/shard_map/while
  163.8 9.2 %copy-start.19 = (bf16[256,512]{1,0:T(8,128)(2,1)S(1)}, bf16[256,512]{1,0:T(8,128)(2,1)}, u32[]{:S(2)}) copy-start(bf16[256,512]{1,0:T(8,128)(2,1)} %param.24) | copy-start | bytes 786436
  177.9 34.3 %all-gather.7.cloned.1.call-start = ((), (), s32[]{:S(2)}) async-start(), calls=%async_computation.6 | async-start | bytes 4374528 | tf_op jit(solution)/shard_map/all_gather | solution.py:133
  199.1 65.6 %reduce-scatter.7.cloned.1.call-start = ((), (), s32[]{:S(2)}) async-start(), calls=%async_computation.7 | async-start | bytes 8749056 | tf_op jit(solution)/shard_map/reduce_scatter | solution.py:138
  212.3 32.2 %copy-start.39 = (bf16[1024,512]{1,0:T(8,128)(2,1)S(1)}, bf16[1024,512]{1,0:T(8,128)(2,1)}, u32[]{:S(2)}) copy-start(bf16[1024,512]{1,0:T(8,128)(2,1)} %param.30) | copy-start | bytes 3145732
  242.0 2.5 copy-start.41
  249.4 42.1 %all-gather.9.cloned.1.call-start = ((), (), s32[]{:S(2)}) async-start(), calls=%async_computation.8 | async-start | bytes 4374528 | tf_op jit(solution)/shard_map/all_gather | solution.py:152
  278.3 46.8 %reduce-scatter.9.cloned.1.call-start = ((), (), s32[]{:S(2)}) async-start(), calls=%async_computation.9 | async-start | bytes 8749056 | tf_op jit(solution)/shard_map/reduce_scatter | solution.py:161
  301.8 2.6 copy-start.42
  309.9 39.6 %all-gather.11.cloned.1.call-start = ((), (), s32[]{:S(2)}) async-start(), calls=%async_computation.10 | async-start | bytes 4374528 | tf_op jit(solution)/shard_map/all_gather | solution.py:168
  336.3 416.7 %reduce-scatter.11.cloned.1.call-start = ((), (), s32[]{:S(2)}) async-start(), calls=%async_computation.11 | async-start | bytes 4374528 | tf_op jit(solution)/shard_map/reduce_scatter | solution.py:194
  447.9 14.9 %copy-start.4 = (bf16[2,1424,4,64]{1,3,2,0:T(8,128)(2,1)S(1)}, bf16[2,1424,4,64]{1,3,2,0:T(8,128)(2,1)}, u32[]{:S(2)}) copy-start(bf16[2,1424,4,64]{1,3,2,0:T(8,128)(2,1)} %copy-done.3) | copy-start | bytes 4374532 | tf_op jit(solution)/shard_map/while
  564.4 14.9 %copy-start.4 = (bf16[2,1424,4,64]{1,3,2,0:T(8,128)(2,1)S(1)}, bf16[2,1424,4,64]{1,3,2,0:T(8,128)(2,1)}, u32[]{:S(2)}) copy-start(bf16[2,1424,4,64]{1,3,2,0:T(8,128)(2,1)} %copy-done.3) | copy-start | bytes 4374532 | tf_op jit(solution)/shard_map/while
  607.0 5.5 copy-start.8
  634.0 2.5 copy-start.40
  640.7 238.3 %all-reduce.5.cloned.1.call-start = ((), (), s32[]{:S(2)}) async-start(), calls=%async_computation.12 | async-start | bytes 12582912 | tf_op jit(solution)/shard_map/psum | solution.py:197
  640.7 8.5 copy-start.37
  640.7 18.2 %slice-start = ((s8[4374528]{0:T(1024)(128)(4,1)}), s8[4194304]{0:T(1024)(128)(4,1)S(1)}, s32[]{:S(2)}) async-start(s8[4374528]{0:T(1024)(128)(4,1)} %bitcast.142), calls=%async_computation.13 | async-start | bytes 8388608
  649.2 7.9 copy-start.9
  649.2 7.9 copy-start.38
  649.2 9.7 %slice-start.1 = ((s8[4374528]{0:T(1024)(128)(4,1)}), s8[180224]{0:T(1024)(128)(4,1)S(1)}, s32[]{:S(2)}) async-start(s8[4374528]{0:T(1024)(128)(4,1)} %bitcast.142), calls=%async_computation.14 | async-start | bytes 360448
  662.9 47.3 %copy-start.26 = (f32[1024]{0:T(1024)S(1)}, f32[1024]{0:T(1024)}, u32[]{:S(2)}) copy-start(f32[1024]{0:T(1024)} %get-tuple-element.280) | copy-start | bytes 12292
  879.0 3.2 copy-start.17
  879.0 4.0 copy-start.16
  883.0 2.6 copy-start.1
  (27 other events, 31.6 us)
Sparse Core Ops, SparseCore 0:
  9.6 14.4 all-gather.4
  178.1 15.0 reduce-scatter.4
  199.2 13.0 all-gather.6
  249.6 15.0 reduce-scatter.6
  278.4 13.0 all-gather.8
  310.1 15.0 reduce-scatter.8
  336.4 13.0 all-gather.10
  640.8 11.6 reduce-scatter.10
  663.0 215.9 all-reduce.4
where the time goes:
time: 898 us; the launch traced here: 892 us
  matrix products  316 us (35%)
  waiting for transfers between devices  219 us (24%)
  other arithmetic  134 us (15%)
  local copies, waits for them, and re-layouts  120 us (13%)
  blocking collectives  87.2 us (10%)
  between operations  14.3 us (2%)
    psum x1, waiting for transfers between devices, per_device(): lax.psum((grad_w_qkv, grad_b_qv, grad_w_out), 'dp')  122 us
    dot_general x4, matrix products, masked_scores(): jnp.einsum('qhd,khd->hqk', queries, key_rows, preferred_element_type=jnp....  89 us
    convert_element_type x2, other arithmetic, attend_backward(): grad_scores = (probs * (grad_probs - jnp.sum(probs * grad_probs, axis=2,...  59 us
    psum x1, blocking collectives, per_device(): lax.psum((grad_b_out, grad_gain_one, grad_shift_one, grad_b_down, grad_ga...  44.4 us
    psum x1, blocking collectives, per_device(): lax.psum((grad_w_qkv, grad_b_qv, grad_w_out), 'dp')  42.8 us
    dot_general x2, matrix products, attend_backward(): jnp.einsum('qhd,khd->hqk', grad_mixed, values, preferred_element_type=jnp...  35.3 us
    another operation x7, local copies, waits for them, and re-layouts, per_device(): jnp.stack([grad_q.reshape(-1, attn_width), grad_k.reshape(-1, attn_width)...  30.7 us
    dot_general x2, matrix products, attend_backward(): jnp.einsum('hqk,qhd->khd', probs.astype(jnp.bfloat16), grad_mixed, prefer...  29.7 us
  transfers between devices with their start and end apart: 9, of which 8 were waited for; matrix products, arithmetic and copies ran while one was open for 3% of the time, Pallas kernels for 0%

commit v1 on v0

v1 whole, which is shorter than its diff:
```python
import jax
import jax.numpy as jnp
from jax import lax
from jax.experimental import pallas as pl
from jax.experimental.pallas import tpu as pltpu
from jax.sharding import PartitionSpec as P

HEAD_DIM = 64
SLOTS = 1424
WIDTHS = (7, 21, 321, 862)
LANES = 1536
CLASSES = 48
BIG = 1e30
EPS = 1e-05
MIB = 2**20

bf16 = jnp.bfloat16
f32 = jnp.float32


def mul(left, right, left_dim=1, right_dim=0):
    return lax.dot_general(
        left, right, (((left_dim,), (right_dim,)), ((), ())), preferred_element_type=f32
    )


def params(limit):
    return pltpu.CompilerParams(vmem_limit_bytes=limit * MIB)


def cover(width, start, stop, last):
    used = SLOTS // width * width
    low = start // width * width
    high = last if stop > used else -(-stop // width) * width
    return (low // 128 * 128, min(-(-min(high, last) // 128) * 128, LANES))


def groups_of(width, rows, step):
    found = []
    for start in range(0, rows, step):
        low, high = cover(width, start, min(start + step, rows), rows)
        if found and found[-1][2] == low and found[-1][2] + found[-1][3] == high:
            first, count = found[-1][:2]
            found[-1] = (first, count + step, low, high - low)
        else:
            found.append((start, step, low, high - low))
    return found


FORWARD = (
    [(128 * i, 128, max(128 * i - 128, 0), min(128 * i + 256, LANES) - max(128 * i - 128, 0)) for i in range(12)],
    groups_of(321, SLOTS, 128),
    [(768, 768, 768, 768), (0, 896, 0, 896)],
)
BACKWARD = (
    FORWARD[0],
    groups_of(321, 1284, 128),
    [(0, 896, 0, 896)],
)


def token_class(width):
    token = lax.broadcasted_iota(jnp.int32, (CLASSES, LANES), 1)
    numbers = token.astype(f32)
    held = jnp.floor((numbers + 0.5) * (1.0 / width)).astype(jnp.int32)
    held = jnp.where(token < SLOTS, held, (SLOTS - 1) // width + 1)
    row = lax.broadcasted_iota(jnp.int32, (CLASSES, LANES), 0)
    return held % CLASSES == row


def write_masks(set_ref, hot_ref, bar_ref):
    for number, width in enumerate(WIDTHS):

        @pl.when(set_ref[0] == number)
        def _():
            same = token_class(width)
            hot_ref[...] = jnp.where(same, 1.0, 0.0).astype(bf16)
            bar_ref[:CLASSES, :] = jnp.where(same, 0.0, -BIG).astype(bf16)

    row = lax.broadcasted_iota(jnp.int32, (16, LANES), 0)
    bar_ref[CLASSES:, :] = jnp.where(row < 3, 1.0, 0.0).astype(bf16)


def split_three(row):
    high = row.astype(bf16)
    rest = row - high.astype(f32)
    middle = rest.astype(bf16)
    low = (rest - middle.astype(f32)).astype(bf16)
    return high, middle, low


def extra_rows(row):
    parts = [p.astype(f32) for p in split_three(row)]
    number = lax.broadcasted_iota(jnp.int32, (16, row.shape[1]), 0)
    held = jnp.where(number == 0, parts[0], jnp.where(number == 1, parts[1], jnp.where(number == 2, parts[2], 0.0)))
    return held.astype(bf16)


def attend_forward(set_ref, x_ref, wa_ref, wb_ref, ba_ref, bb_ref, q_ref, k_ref, v_ref, o_ref, lse_ref, xt_ref, hot_ref, bar_ref):
    write_masks(set_ref, hot_ref, bar_ref)
    tail = jnp.zeros((LANES - SLOTS, x_ref.shape[1]), bf16)
    xt_ref[...] = jnp.concatenate([x_ref[...], tail], axis=0).T
    for side, (w_ref, b_ref) in enumerate(((wa_ref, ba_ref), (wb_ref, bb_ref))):
        for kind, out_ref in enumerate((q_ref, k_ref, v_ref)):
            weight = w_ref[kind].T
            rows = weight.shape[0]
            if kind != 1:
                row = b_ref[kind // 2 : kind // 2 + 1, :].astype(f32)
                column = jnp.broadcast_to(row, (128, rows)).T
                column = jnp.concatenate([column] * 4, axis=1)
            for start in range(0, LANES, 512):
                part = mul(weight, xt_ref[:, start : start + 512])
                if kind != 1:
                    part = part + column
                if kind == 0:
                    part = part * 0.125
                out_ref[side * rows : (side + 1) * rows, start : start + 512] = part.astype(bf16)

    def one_head(head, groups):
        rows = pl.ds(pl.multiple_of(head * 64, 64), 64)
        keep = None
        for q0, nq, k0, nk in groups:
            keys = jnp.concatenate([k_ref[rows, k0 : k0 + nk], bar_ref[:, k0 : k0 + nk]], axis=0).T
            ones = jnp.ones((16, nk), bf16)
            vals = jnp.concatenate([v_ref[rows, k0 : k0 + nk], ones], axis=0)
            for start in range(q0, q0 + nq, 256):
                size = min(256, q0 + nq - start)
                lanes = slice(start, start + size)
                zeros = jnp.zeros((16, size), bf16)
                quer = jnp.concatenate([q_ref[rows, lanes], hot_ref[:, lanes], zeros], axis=0)
                scores = mul(keys, quer)
                top = jnp.max(scores, axis=0, keepdims=True)
                raised = jnp.exp(scores - top).astype(bf16)
                total = mul(vals, raised)
                sums = total[64:65, :]
                mixed = (total[:64, :] * (1.0 / sums)).astype(bf16)
                logs = top + jnp.log(sums)
                if len(groups) == 2 and start == 768:
                    if q0 == 768:
                        keep = (mixed[:, :128], logs[:, :128])
                    else:
                        lane = lax.broadcasted_iota(jnp.int32, (64, 128), 1)
                        mixed = jnp.where(lane < WIDTHS[3] - 768, mixed.astype(f32), keep[0].astype(f32)).astype(bf16)
                        logs = jnp.where(lane[:1] < WIDTHS[3] - 768, logs, keep[1])
                o_ref[rows, lanes] = mixed
                lse_ref[pl.ds(pl.multiple_of(head * 16, 16), 16), lanes] = extra_rows(-logs)

    for group in range(3):
        chosen = (set_ref[0] < 2, set_ref[0] == 2, set_ref[0] == 3)[group]

        @pl.when(chosen)
        def _():
            def pair(number, carry):
                one_head(2 * number, FORWARD[group])
                one_head(2 * number + 1, FORWARD[group])
                return carry

            lax.fori_loop(0, q_ref.shape[0] // 128, pair, 0)


def attend_backward(set_ref, q_ref, k_ref, v_ref, g_ref, lse_ref, delta_ref, dq_ref, dk_ref, dv_ref, hot_ref, bar_ref, p_ref, s_ref, ka_ref, va_ref):
    write_masks(set_ref, hot_ref, bar_ref)

    def one_head(head, groups, slot):
        rows = pl.ds(pl.multiple_of(head * 64, 64), 64)
        more = pl.ds(pl.multiple_of(head * 16, 16), 16)
        single = len(groups) == 1
        if not single:
            ka_ref[...] = jnp.zeros_like(ka_ref)
            va_ref[...] = jnp.zeros_like(va_ref)
        for q0, nq, k0, nk in groups:
            span = slice(k0, k0 + nk)
            held = slice(q0, q0 + nq)
            keys = jnp.concatenate([k_ref[rows, span], bar_ref[:, span]], axis=0)
            vals = jnp.concatenate([v_ref[rows, span], bar_ref[CLASSES:, span]], axis=0)
            for start in range(q0, q0 + nq, 256):
                size = min(256, q0 + nq - start)
                lanes = slice(start, start + size)
                quer = jnp.concatenate(
                    [q_ref[rows, lanes], hot_ref[:, lanes], lse_ref[more, lanes]], axis=0
                )
                grad = jnp.concatenate([g_ref[rows, lanes], delta_ref[more, lanes]], axis=0)
                probs = jnp.exp(mul(quer, keys, 0, 0))
                slopes = probs * mul(grad, vals, 0, 0)
                p_ref[slot, start - q0 : start - q0 + size, :nk] = probs.astype(bf16)
                s_ref[slot, start - q0 : start - q0 + size, :nk] = slopes.astype(bf16)
            dv = mul(g_ref[rows, held], p_ref[slot, :nq, :nk])
            dk = mul(q_ref[rows, held], s_ref[slot, :nq, :nk])
            dq = mul(k_ref[rows, span], s_ref[slot, :nq, :nk], 1, 1)
            dq_ref[rows, held] = (dq * 0.125).astype(bf16)
            if single:
                dv_ref[rows, span] = dv.astype(bf16)
                dk_ref[rows, span] = dk.astype(bf16)
            else:
                va_ref[:, span] += dv
                ka_ref[:, span] += dk
        if single:
            rest = LANES - 896
            for out in (dq_ref, dk_ref, dv_ref):
                out[rows, 896:] = jnp.zeros((64, rest), bf16)
        else:
            dv_ref[rows, :] = va_ref[...].astype(bf16)
            dk_ref[rows, :] = ka_ref[...].astype(bf16)
            done = groups[-1][0] + groups[-1][1]
            if done < LANES:
                dq_ref[rows, done:] = jnp.zeros((64, LANES - done), bf16)

    for group in range(3):
        chosen = (set_ref[0] < 2, set_ref[0] == 2, set_ref[0] == 3)[group]

        @pl.when(chosen)
        def _():
            def pair(number, carry):
                one_head(2 * number, BACKWARD[group], 0)
                one_head(2 * number + 1, BACKWARD[group], 1)
                return carry

            lax.fori_loop(0, q_ref.shape[0] // 128, pair, 0)


TILES = [(i * 256, 256) for i in range(5)] + [(1280, 144)]


def over_tiles(step):
    def body(number, carry):
        step(pl.multiple_of(number * 256, 256), 256)
        return carry

    lax.fori_loop(0, 5, body, 0)
    step(1280, 144)


def mean_of(matrix):
    return jnp.sum(matrix, axis=1, keepdims=True) * (1.0 / matrix.shape[1])


def norm_parts(matrix):
    centre = matrix - mean_of(matrix)
    spread = lax.rsqrt(mean_of(centre * centre) + EPS)
    return centre * spread, spread


def norm_back(scaled, normed, spread):
    return spread * (scaled - mean_of(scaled) - normed * mean_of(scaled * normed))


def fold(matrix):
    return jnp.sum(matrix.reshape(matrix.shape[0] // 8, 8, matrix.shape[1]), axis=0)


def gelu_parts(pre):
    size = jnp.abs(pre)
    t = 1.0 / (1.0 + (0.3275911 * 2.0**-0.5) * size)
    bell = jnp.exp(-0.5 * pre * pre)
    poly = 0.5 * 1.061405429
    for factor in (-1.453152027, 1.421413741, -0.284496736, 0.254829592):
        poly = poly * t + 0.5 * factor
    tail = poly * t * bell
    phi = jnp.where(pre > 0, 1.0 - tail, tail)
    return pre * phi, phi + pre * (bell * (2.0 * jnp.pi) ** -0.5)


HIDDEN_STEP = 512


def feed_forward(
    set_ref, x_ref, o_ref, wo_a, wo_b, ua_ref, ub_ref, bup_ref, da_ref, db_ref, vec_ref, cot_ref,
    out_ref, hid_ref, res_ref, slope_ref, sec_ref, gd_a, gd_b, sums_ref, act_ref, low_ref,
):
    width = x_ref.shape[1]
    half = ua_ref.shape[1]
    used = jnp.where(set_ref[0] == 0, SLOTS // 7 * 7, jnp.where(set_ref[0] == 1, SLOTS // 21 * 21, jnp.where(set_ref[0] == 2, SLOTS // 321 * 321, 862)))
    sums_ref[...] = jnp.zeros_like(sums_ref)
    b_out, gain_one, shift_one, b_down, gain_two, shift_two = (vec_ref[i : i + 1, :].astype(f32) for i in range(6))

    def step(start, size):
        rows = pl.ds(start, size)
        lanes = pl.ds(start, 256)
        split = wo_a.shape[0]
        attn = mul(o_ref[:split, lanes], wo_a[...], 0, 0) + mul(o_ref[split:, lanes], wo_b[...], 0, 0)
        resid = x_ref[rows, :].astype(f32) + attn[:size] + b_out
        res_ref[rows, :] = resid
        normed, _ = norm_parts(resid)
        hidden = normed * gain_one + shift_one
        low = hidden.astype(bf16)
        hid_ref[rows, :] = low
        total = None
        for side, (u_ref, d_ref) in enumerate(((ua_ref, da_ref), (ub_ref, db_ref))):
            for at in range(0, half, HIDDEN_STEP):
                place = slice(side * half + at, side * half + at + HIDDEN_STEP)
                pre = mul(low, u_ref[:, at : at + HIDDEN_STEP]) + bup_ref[:, place].astype(f32)
                active, slope = gelu_parts(pre)
                active = active.astype(bf16)
                act_ref[rows, place] = active
                slope_ref[rows, place] = slope.astype(bf16)
                part = mul(active, d_ref[at : at + HIDDEN_STEP, :])
                total = part if total is None else total + part
        second = hidden + total + b_down
        normed, spread = norm_parts(second)
        out_ref[rows, :] = (normed * gain_two + shift_two).astype(bf16)
        row = start + lax.broadcasted_iota(jnp.int32, (size, width), 0)
        top = jnp.where(row < used, cot_ref[rows, :].astype(f32), 0.0)
        grad = norm_back(top * gain_two, normed, spread)
        sec_ref[rows, :] = grad
        low_ref[rows, :] = grad.astype(bf16)
        sums_ref[0:8, :] += fold(top * normed)
        sums_ref[8:16, :] += fold(top)
        sums_ref[16:24, :] += fold(grad)

    over_tiles(step)
    for side, g_ref in enumerate((gd_a, gd_b)):
        for at in range(0, half, 256):
            place = slice(side * half + at, side * half + at + 256)
            g_ref[at : at + 256, :] = mul(act_ref[:, place], low_ref[...], 0, 0).astype(g_ref.dtype)


def feed_backward(
    sec_ref, slope_ref, hid_ref, res_ref, o_ref, wo_a, wo_b, ua_ref, ub_ref, da_ref, db_ref, vec_ref,
    gr_ref, g_ref, delta_ref, gu_a, gu_b, go_a, go_b, sums_ref, bup_ref, pre_ref, mix_ref,
):
    half = ua_ref.shape[1]
    sums_ref[...] = jnp.zeros_like(sums_ref)
    bup_ref[...] = jnp.zeros_like(bup_ref)
    gain_one = vec_ref[1:2, :].astype(f32)
    mix_ref[SLOTS:, :] = jnp.zeros((LANES - SLOTS, mix_ref.shape[1]), bf16)

    def step(start, size):
        rows = pl.ds(start, size)
        second = sec_ref[rows, :]
        low = second.astype(bf16)
        total = None
        for side, (u_ref, d_ref) in enumerate(((ua_ref, da_ref), (ub_ref, db_ref))):
            for at in range(0, half, HIDDEN_STEP):
                place = slice(side * half + at, side * half + at + HIDDEN_STEP)
                inner = mul(low, d_ref[at : at + HIDDEN_STEP, :], 1, 1)
                pre = (inner * slope_ref[rows, place].astype(f32)).astype(bf16)
                pre_ref[rows, place] = pre
                bup_ref[:, place] += fold(pre.astype(f32))
                part = mul(pre, u_ref[:, at : at + HIDDEN_STEP], 1, 1)
                total = part if total is None else total + part
        hidden = second + total
        normed, spread = norm_parts(res_ref[rows, :])
        grad = norm_back(hidden * gain_one, normed, spread)
        gr_ref[rows, :] = grad
        mix_ref[rows, :] = grad.astype(bf16)
        sums_ref[0:8, :] += fold(hidden * normed)
        sums_ref[8:16, :] += fold(hidden)
        sums_ref[16:24, :] += fold(grad)

    over_tiles(step)
    for side, out in enumerate((gu_a, gu_b)):
        for at in range(0, half, 256):
            place = slice(side * half + at, side * half + at + 256)
            out[:, at : at + 256] = mul(hid_ref[...], pre_ref[:, place], 0, 0).astype(out.dtype)
    split = wo_a.shape[0]
    for side, (out, w_ref) in enumerate(((go_a, wo_a), (go_b, wo_b))):
        place = slice(side * split, (side + 1) * split)
        out[...] = mul(o_ref[place, :], mix_ref[...]).astype(out.dtype)
        for start in range(0, LANES, 512):
            lanes = slice(start, start + 512)
            grad = mul(w_ref[...], mix_ref[lanes, :], 1, 1).astype(bf16)
            g_ref[place, lanes] = grad
            prod = grad.astype(f32) * o_ref[place, lanes].astype(f32)
            for head in range(split // 64):
                at = (side * (split // 64) + head) * 16
                delta = jnp.sum(prod[head * 64 : head * 64 + 64], axis=0, keepdims=True)
                delta_ref[at : at + 16, lanes] = extra_rows(-delta)


def project_backward(x_ref, dq_ref, dk_ref, dv_ref, wa_ref, wb_ref, gr_ref, gi_ref, ga_ref, gb_ref, sums_ref, xt_ref, wt_ref):
    tail = jnp.zeros((LANES - SLOTS, x_ref.shape[1]), bf16)
    xt_ref[...] = jnp.concatenate([x_ref[...], tail], axis=0).T
    rows = wa_ref.shape[2]
    ones = jnp.ones((8, LANES), bf16)
    for side, (w_ref, g_ref) in enumerate(((wa_ref, ga_ref), (wb_ref, gb_ref))):
        place = slice(side * rows, (side + 1) * rows)
        for kind, d_ref in enumerate((dq_ref, dk_ref, dv_ref)):
            g_ref[kind] = mul(xt_ref[...], d_ref[place, :], 1, 1).astype(g_ref.dtype)
            wt_ref[kind, place, :] = w_ref[kind].T
            if kind != 1:
                sums_ref[kind // 2, :, place] = mul(ones, d_ref[place, :], 1, 1)
    for start in range(0, SLOTS, 256):
        size = min(256, SLOTS - start)
        lanes = slice(start, start + 256)
        total = mul(dq_ref[:, lanes], wt_ref[0], 0, 0)
        total = total + mul(dk_ref[:, lanes], wt_ref[1], 0, 0)
        total = total + mul(dv_ref[:, lanes], wt_ref[2], 0, 0)
        gi_ref[start : start + size, :] = gr_ref[start : start + size, :] + total[:size]


def shape(dims, kind=bf16):
    return jax.ShapeDtypeStruct(dims, kind)


smem = pl.BlockSpec(memory_space=pltpu.SMEM)


def specs(count):
    return [smem] + [pl.BlockSpec(memory_space=pltpu.VMEM)] * (count - 1)


def call_forward(number, x, wa, wb, ba, bb):
    width = 2 * wa.shape[2]
    big = shape((width, LANES))
    return pl.pallas_call(
        attend_forward, name="attend_forward",
        out_shape=[big, big, big, big, shape((width // 4, LANES))],
        in_specs=specs(6),
        scratch_shapes=[pltpu.VMEM((x.shape[1], LANES), bf16), pltpu.VMEM((CLASSES, LANES), bf16), pltpu.VMEM((64, LANES), bf16)],
        compiler_params=params(40),
    )(number, x, wa, wb, ba, bb)


def call_feed_forward(number, x, mixed, wo_a, wo_b, up_a, up_b, b_up, down_a, down_b, vecs, cot):
    rows, width = x.shape
    half = up_a.shape[1]
    return pl.pallas_call(
        feed_forward, name="feed_forward",
        out_shape=[
            shape((rows, width)), shape((rows, width)), shape((rows, width), f32), shape((rows, 2 * half)),
            shape((rows, width), f32), shape((half, width)), shape((half, width)), shape((24, width), f32),
        ],
        in_specs=specs(12),
        scratch_shapes=[pltpu.VMEM((rows, 2 * half), bf16), pltpu.VMEM((rows, width), bf16)],
        compiler_params=params(56),
    )(number, x, mixed, wo_a, wo_b, up_a, up_b, b_up, down_a, down_b, vecs, cot)


def call_feed_backward(second, slope, hidden, resid, mixed, wo_a, wo_b, up_a, up_b, down_a, down_b, vecs):
    rows, width = second.shape
    half = up_a.shape[1]
    split = wo_a.shape[0]
    return pl.pallas_call(
        feed_backward, name="feed_backward",
        out_shape=[
            shape((rows, width), f32), shape((2 * split, LANES)), shape((2 * split // 4, LANES)),
            shape((width, half)), shape((width, half)), shape((split, width)), shape((split, width)),
            shape((24, width), f32), shape((8, 2 * half), f32),
        ],
        scratch_shapes=[pltpu.VMEM((rows, 2 * half), bf16), pltpu.VMEM((LANES, width), bf16)],
        compiler_params=params(56),
    )(second, slope, hidden, resid, mixed, wo_a, wo_b, up_a, up_b, down_a, down_b, vecs)


def call_backward(number, q, k, v, grad, lse, delta):
    big = shape(q.shape)
    return pl.pallas_call(
        attend_backward, name="attend_backward",
        out_shape=[big, big, big],
        in_specs=specs(7),
        scratch_shapes=[
            pltpu.VMEM((CLASSES, LANES), bf16), pltpu.VMEM((64, LANES), bf16),
            pltpu.VMEM((2, 896, 896), bf16), pltpu.VMEM((2, 896, 896), bf16),
            pltpu.VMEM((64, LANES), f32), pltpu.VMEM((64, LANES), f32),
        ],
        compiler_params=params(40),
    )(number, q, k, v, grad, lse, delta)


def call_project(x, dq, dk, dv, wa, wb, resid):
    rows, width = x.shape
    return pl.pallas_call(
        project_backward, name="project_backward",
        out_shape=[shape((rows, width), f32), shape(wa.shape), shape(wb.shape), shape((2, 8, 2 * wa.shape[2]), f32)],
        scratch_shapes=[pltpu.VMEM((width, LANES), bf16), pltpu.VMEM((3, 2 * wa.shape[2], width), bf16)],
        compiler_params=params(40),
    )(x, dq, dk, dv, wa, wb, resid)


def swap(array):
    return lax.ppermute(array, "mp", [(0, 1), (1, 0)])


def per_device(
    variates, dataset, w_qkv, b_qv, w_out, b_out, gain_one, shift_one, w_up, b_up, w_down, b_down, gain_two, shift_two, cotangent,
):
    side = lax.axis_index("mp")
    number = lax.dynamic_slice_in_dim(dataset, side, 1, 0)
    width, half = w_up.shape
    small = swap(jnp.concatenate([b_qv.reshape(-1), b_up]).reshape(3, -1))
    other_b_qv = small[0:1].reshape(b_qv.shape) if small.shape[1] == b_qv.size else small.reshape(-1)[: b_qv.size].reshape(b_qv.shape)
    other_b_up = small.reshape(-1)[b_qv.size :]
    other_qkv = swap(w_qkv)
    other_out, other_up, other_down = swap(w_out), swap(w_up), swap(w_down)
    vecs = jnp.stack([b_out, gain_one, shift_one, b_down, gain_two, shift_two, b_out, b_out])
    b_up_all = jnp.concatenate([b_up, other_b_up])[None]
    q, k, v, mixed, lse = call_forward(number, variates, w_qkv, other_qkv, b_qv, other_b_qv)
    out, hidden, resid, slope, second, gd_a, gd_b, sums_two = call_feed_forward(
        number, variates, mixed, w_out, other_out, w_up, other_up, b_up_all, w_down, other_down, vecs, cotangent
    )
    own_down = lax.psum(gd_a + swap(gd_b), "dp")
    grad_res, grad_mix, delta, gu_a, gu_b, go_a, go_b, sums_one, bup_sum = call_feed_backward(
        second, slope, hidden, resid, mixed, w_out, other_out, w_up, other_up, w_down, other_down, vecs
    )
    vectors = jnp.concatenate(
        [jnp.sum(part.reshape(3, 8, width), axis=1).reshape(-1) for part in (sums_two, sums_one)]
    )
    bup_flat = jnp.sum(bup_sum, axis=0)
    own_up, own_out = lax.psum((gu_a + swap(gu_b), go_a + swap(go_b)), "dp")
    dq, dk, dv = call_backward(number, q, k, v, grad_mix, lse, delta)
    grad_in, gq_a, gq_b, bqv = call_project(variates, dq, dk, dv, w_qkv, other_qkv, grad_res)
    bqv = bqv[:, 0]
    split = b_qv.shape[1]
    mine = jnp.concatenate([bup_flat[:half], bqv[:, :split].reshape(-1)])
    theirs = jnp.concatenate([bup_flat[half:], bqv[:, split:].reshape(-1)])
    own_qkv = lax.psum(gq_a + swap(gq_b), "dp")
    vectors = vectors + swap(vectors)
    mine = mine + swap(theirs)
    count = vectors.shape[0]
    total = lax.psum(jnp.concatenate([vectors, mine]), "dp")
    vec = total[:count].reshape(6, width)
    rest = total[count:]
    return (
        out, grad_in, own_qkv.astype(f32), rest[half:].reshape(2, split), own_out.astype(f32),
        vec[5], vec[3], vec[4], own_up.astype(f32), rest[:half], own_down.astype(f32), vec[2], vec[0], vec[1],
    )


def solution(mesh):
    wide = P(("dp", "mp"), None)
    weights = (P(None, None, "mp"), P(None, "mp"), P("mp", None))
    placed = (wide, P("dp"), *weights, P(), P(), P(), P(None, "mp"), P("mp"), P("mp", None), P(), P(), P(), wide)
    given = (wide, wide, *weights, P(), P(), P(), P(None, "mp"), P("mp"), P("mp", None), P(), P(), P())
    return jax.shard_map(per_device, mesh=mesh, in_specs=placed, out_specs=given, check_vma=False)
```

time: 898 us -> 330 us (0.37)
  matrix products: 316 us -> 0 us
  waiting for transfers between devices: 219 us -> 72.9 us
  Pallas kernels: 0 us -> 124 us
  other arithmetic: 134 us -> 13.4 us
  local copies, waits for them, and re-layouts: 120 us -> 17.6 us
    dot_general x26 -> x0, matrix products: 316 us -> none  [the longest x4 89 us: masked_scores(): jnp.einsum('qhd,khd->hqk', queries, key_rows, preferred_element_type=jnp....]
    pallas_call x0 -> x5, Pallas kernels: none -> 124 us  [the longest x1 38 us: call_forward(): pl.pallas_call(attend_forward, name='attend_forward', out_shape=[big, big...]
    convert_element_type x15 -> x4, other arithmetic: 69.4 us -> 7.48 us  [the longest x1 2.41 us: per_device(): own_qkv.astype(f32)]
    all_gather x4 -> x0, waiting for transfers between devices: 53 us -> none  [the longest x1 13.6 us: per_device(): source = lax.all_gather(variates, 'mp', axis=0, tiled=True)]
    reduce_sum x13 -> x3, other arithmetic: 52.5 us -> 0.07 us  [the longest x2 0.05 us: per_device(): jnp.sum(part.reshape(3, 8, width), axis=1).reshape(-1)]
    psum x1, waiting for transfers between devices: 122 us -> 69.9 us  [per_device(): own_qkv = lax.psum(gq_a + swap(gq_b), 'dp')]
    reduce_scatter x4 -> x0, waiting for transfers between devices: 44 us -> none  [the longest x1 15.2 us: per_device(): grad_mid = lax.psum_scatter(mid_part, 'mp', scatter_dimension=0, tiled=True)]
    another operation x13 -> x7, local copies, waits for them, and re-layouts: 36 us -> 4.72 us  [per_device(): jnp.stack([b_out, gain_one, shift_one, b_down, gain_two, shift_two, b_out...]
  transfers between devices with their start and end apart: 9 -> 12, of which waited for: 8 -> 4; matrix products, arithmetic and copies ran while one was open for 3% -> 4% of each run, Pallas kernels for 0% -> 29%
where the time goes in v1:
time: 330 us; the launch traced here: 328 us
  Pallas kernels  124 us (38%)
  blocking collectives  81.7 us (25%)
  waiting for transfers between devices  72.9 us (22%)
  local copies, waits for them, and re-layouts  17.6 us (5%)
  between operations  14.5 us (4%)
  other arithmetic  13.4 us (4%)
  starting transfers between devices  3.35 us (1%)
    psum x1, blocking collectives, per_device(): total = lax.psum(jnp.concatenate([vectors, mine]), 'dp')  81.7 us
    psum x1, waiting for transfers between devices, per_device(): own_qkv = lax.psum(gq_a + swap(gq_b), 'dp')  69.9 us
    pallas_call x1, Pallas kernels, call_forward(): pl.pallas_call(attend_forward, name='attend_forward', out_shape=[big, big...  38 us
    pallas_call x1, Pallas kernels, call_feed_forward(): pl.pallas_call(feed_forward, name='feed_forward', out_shape=[shape((rows,...  29.2 us
    pallas_call x1, Pallas kernels, call_backward(): pl.pallas_call(attend_backward, name='attend_backward', out_shape=[big, b...  25.2 us
    pallas_call x1, Pallas kernels, call_feed_backward(): pl.pallas_call(feed_backward, name='feed_backward', out_shape=[shape((row...  24 us
    unnamed x46, local copies, waits for them, and re-layouts  9.2 us
    pallas_call x1, Pallas kernels, call_project(): pl.pallas_call(project_backward, name='project_backward', out_shape=[shap...  7.59 us
  transfers between devices with their start and end apart: 12, of which 4 were waited for; matrix products, arithmetic and copies ran while one was open for 4% of the time, Pallas kernels for 29%

profile of v1, /device:TPU:0, one launch (start us, length us, event | category | flops | bytes accessed | tf_op | source)
XLA Modules:
  0.0 327.5 jit_solution(8240474934478033230)
XLA Ops:
  8.3 0.7 copy.30
  8.9 0.7 pad_maximum_fusion.2
  10.2 0.7 stack.23
  10.9 0.7 stack.24
  11.6 0.7 stack.25
  12.3 0.7 stack.26
  12.9 0.7 stack.27
  14.3 1.2 dynamic_slice.3.set_ref
  16.2 0.7 pad_maximum_fusion.3
  17.5 1.4 copy-done
  18.9 1.1 copy-done.3
  20.7 38.0 %attend_forward.1 = (bf16[512,1536]{1,0:T(8,128)(2,1)S(1)}, bf16[512,1536]{1,0:T(8,128)(2,1)S(1)}, bf16[512,1536]{1,0:T(8,128)(2,1)S(1)}, bf16[512,1536]{1,0:T(8,128)(2,1)S(1)}, bf16[128,1536]{1,0:T(8,128)(2,1)S(1)}) custom-call(s32[1]{0:T(128)} %dynamic_slice.3.set_ref, bf16[1424,512]{1,0:T(8,128)(2,1)S(1)} %copy-done, bf16[3,512,256]{2,1,0:T(8,128)(2,1)S(1)} %copy-done.3, ...), custom_call_target="tpu_custom_call" | custom-call | tf_op jit(solution)/shard_map/attend_forward/pallas_call | solution.py:405
  58.7 1.1 copy-done.2
  59.9 1.0 copy-done.9
  60.9 29.2 %feed_forward.1 = (bf16[1424,512]{1,0:T(8,128)(2,1)}, bf16[1424,512]{1,0:T(8,128)(2,1)}, f32[1424,512]{1,0:T(8,128)}, bf16[1424,2048]{1,0:T(8,128)(2,1)}, f32[14...) custom-call(s32[1]{0:T(128)} %dynamic_slice.3.set_ref, ...), custom_call_target="tpu_custom_call" | custom-call | tf_op jit(solution)/shard_map/feed_forward/pallas_call | solution.py:417
  90.1 24.0 %feed_backward.1 = (f32[1424,512]{1,0:T(8,128)}, bf16[512,1536]{1,0:T(8,128)(2,1)}, bf16[128,1536]{1,0:T(8,128)(2,1)}, bf16[512,1024]{1,0:T(8,128)(2,1)}, bf16[5...) custom-call(f32[1424,512]{1,0:T(8,128)} %get-tuple-element.48.sec_re, ...), custom_call_target="tpu_custom_call" | custom-call | tf_op jit(solution)/shard_map/feed_backward/pallas_call | solution.py:433
  114.6 1.4 copy-done.6
  116.1 1.0 copy-done.7
  117.1 25.2 %attend_backward.1 = (bf16[512,1536]{1,0:T(8,128)(2,1)S(1)}, bf16[512,1536]{1,0:T(8,128)(2,1)S(1)}, bf16[512,1536]{1,0:T(8,128)(2,1)S(1)}) custom-call(s32[1]{0:T(128)} %dynamic_slice.3.set_ref, bf16[512,1536]{1,0:T(8,128)(2,1)S(1)} %get-tuple-element.45.q_ref, bf16[512,1536]{1,0:T(8,128)(2,1)S(1)} %get-tuple-element.46.k_ref, ...), custom_call_target="tpu_custom_call" | custom-call | tf_op jit(solution)/shard_map/attend_backward/pallas_call | solution.py:447
  142.3 7.6 %project_backward.1 = (f32[1424,512]{1,0:T(8,128)}, bf16[3,512,256]{2,1,0:T(8,128)(2,1)S(1)}, bf16[3,512,256]{2,1,0:T(8,128)(2,1)S(1)}, f32[2,8,512]{2,1,0:T(8,128)S(1)}) custom-call(bf16[1424,512]{1,0:T(8,128)(2,1)S(1)} %copy-done.1, bf16[512,1536]{1,0:T(8,128)(2,1)S(1)} %get-tuple-element.55.dq_ref, bf16[512,1536]{1,0:T(8,128)(2,1)S(1)} %get-tuple-element.56.dk_ref, ...), custom_call_target="tpu_custom_call" | custom-call | tf_op jit(solution)/shard_map/project_backward/pallas_call | solution.py:462
  150.4 2.1 collective-permute-done.8
  152.6 0.8 add.35
  153.3 1.1 add.32
  154.4 1.3 add.37
  155.7 1.4 add.36
  157.1 0.8 copy-done.16
  159.6 81.7 %psum.36 = f32[4608]{0:T(1024)S(1)} all-reduce(f32[4608]{0:T(1024)S(1)} %pad_maximum_fusion), channel_id=1, replica_groups=mesh['dp'=16,'mp'=2] {'dp'}, use_global_device_ids=true, to_apply=%region_4.0 | all-reduce | flops 4608 | bytes 36864 | tf_op jit(solution)/shard_map/psum | solution.py:510
  243.1 69.9 %all-reduce.3.cloned.1.call-done = (bf16[3,512,256]{2,1,0:T(8,128)(2,1)}, bf16[256,512]{1,0:T(8,128)(2,1)}, bf16[512,1024]{1,0:T(8,128)(2,1)}, bf16[1024,512]{1,0:T(8,128)(2,1)}) async-done(((bf16[3,512,256]{2,1,0:T(8,128)(2,1)}, bf16[256,512]{1,0:T(8,128)(2,1)}, bf16[512,1024]{1,0:T(8,128)(2,1)}, bf16[1024,512]{1,0:T(8,128)(2,1)}), (bf16[3,512,256]{2,1,0:T(8,128)(2,1)}, bf16[256,512]{1,0:T(8,128)(2,1)}, ...) | async-done | bytes 3145744 | tf_op jit(solution)/shard_map/psum | solution.py:506
  313.0 1.9 convert_element_type.13
  314.9 2.4 convert_element_type.12
  317.3 1.6 convert_element_type.14
  318.9 1.6 convert_element_type.15
  (83 shorter events, 8.9 us)
Async XLA Ops:
  7.2 305.8 %all-reduce.3.cloned.1.call-start = ((), (), s32[]{:S(2)}) async-start(), calls=%async_computation | async-start | bytes 6291456 | tf_op jit(solution)/shard_map/psum | solution.py:506
  7.2 52.7 %collective-permute-start.3 = (bf16[512,1024]{1,0:T(8,128)(2,1)}, bf16[512,1024]{1,0:T(8,128)(2,1)S(1)}, u32[]{:S(2)}, u32[]{:S(2)}) collective-permute-start(bf16[512,1024]{1,0:T(8,128)(2,1)} %ua_ref.3), channel_id=1, source_target_pairs={{0,1},{1,0},{2,3},{3,2},{4,5},{5,4},{6,7},{7,6},{8,9},{9,8},{10,11... | collective-permute-start | bytes 3145736 | tf_op jit(solution)/shard_map/ppermute | solution.py:471
  7.7 52.1 %collective-permute-start.4 = (bf16[1024,512]{1,0:T(8,128)(2,1)}, bf16[1024,512]{1,0:T(8,128)(2,1)}, u32[]{:S(2)}, u32[]{:S(2)}) collective-permute-start(bf16[1024,512]{1,0:T(8,128)(2,1)} %da_ref.3), channel_id=1, source_target_pairs={{0,1},{1,0},{2,3},{3,2},{4,5},{5,4},{6,7},{7,6},{8,9},{9,8},{10,11... | collective-permute-start | bytes 3145736 | tf_op jit(solution)/shard_map/ppermute | solution.py:471
  7.8 9.7 %collective-permute-start = (bf16[3,512,256]{2,1,0:T(8,128)(2,1)}, bf16[3,512,256]{2,1,0:T(8,128)(2,1)S(1)}, u32[]{:S(2)}, u32[]{:S(2)}) collective-permute-start(bf16[3,512,256]{2,1,0:T(8,128)(2,1)} %wa_ref.3), channel_id=1, source_target_pairs={{0,1},{1,0},{2,3},{3,2},{4,5},{5,4},{6,7},{7,6},{8,9},{9,8},{10,11... | collective-permute-start | bytes 2359304 | tf_op jit(solution)/shard_map/ppermute | solution.py:471
  9.6 6.5 %collective-permute-start.1 = (bf16[3,512]{1,0:T(4,128)(2,1)S(1)}, bf16[3,512]{1,0:T(4,128)(2,1)S(1)}, u32[]{:S(2)}, u32[]{:S(2)}) collective-permute-start(bf16[3,512]{1,0:T(4,128)(2,1)S(1)} %reshape.80), channel_id=1, source_target_pairs={{0,1},{1,0},{2,3},{3,2},{4,5},{5,4},{6,7},{7,6},{8,9},{9,8},{10,11... | collective-permute-start | bytes 9224 | tf_op jit(solution)/shard_map/ppermute | solution.py:471
  9.8 50.1 %collective-permute-start.2 = (bf16[256,512]{1,0:T(8,128)(2,1)}, bf16[256,512]{1,0:T(8,128)(2,1)}, u32[]{:S(2)}, u32[]{:S(2)}) collective-permute-start(bf16[256,512]{1,0:T(8,128)(2,1)} %wo_a.3), channel_id=1, source_target_pairs={{0,1},{1,0},{2,3},{3,2},{4,5},{5,4},{6,7},{7,6},{8,9},{9,8},{10,11... | collective-permute-start | bytes 786440 | tf_op jit(solution)/shard_map/ppermute | solution.py:471
  17.5 1.4 copy-start
  18.9 1.1 copy-start.3
  20.0 0.7 copy-start.8
  58.7 1.1 copy-start.2
  59.9 1.0 copy-start.9
  90.1 64.4 %collective-permute-start.10 = (bf16[1024,512]{1,0:T(8,128)(2,1)}, bf16[1024,512]{1,0:T(8,128)(2,1)S(1)}, u32[]{:S(2)}, u32[]{:S(2)}) collective-permute-start(bf16[1024,512]{1,0:T(8,128)(2,1)} %get-tuple-element.71), channel_id=1, source_target_pairs={{0,1},{1,0},{2,3},{3,2},{4,5},{5,4},{6,7},{7,6},{8,9},{9,8},{10,11... | collective-permute-start | bytes 3145736 | tf_op jit(solution)/shard_map/ppermute | solution.py:471
  114.2 41.6 %collective-permute-start.9 = (bf16[512,1024]{1,0:T(8,128)(2,1)}, bf16[512,1024]{1,0:T(8,128)(2,1)S(1)}, u32[]{:S(2)}, u32[]{:S(2)}) collective-permute-start(bf16[512,1024]{1,0:T(8,128)(2,1)} %get-tuple-element.69), channel_id=1, source_target_pairs={{0,1},{1,0},{2,3},{3,2},{4,5},{5,4},{6,7},{7,6},{8,9},{9,8},{10,11... | collective-permute-start | bytes 3145736 | tf_op jit(solution)/shard_map/ppermute | solution.py:471
  114.6 1.4 copy-start.6
  116.1 1.0 copy-start.7
  117.0 25.2 %copy-start.1 = (bf16[1424,512]{1,0:T(8,128)(2,1)S(1)}, bf16[1424,512]{1,0:T(8,128)(2,1)}, u32[]{:S(2)}) copy-start(bf16[1424,512]{1,0:T(8,128)(2,1)} %x_ref.5) | copy-start | bytes 4374532
  117.1 25.2 %copy-start.4 = (bf16[3,512,256]{2,1,0:T(8,128)(2,1)S(1)}, bf16[3,512,256]{2,1,0:T(8,128)(2,1)}, u32[]{:S(2)}) copy-start(bf16[3,512,256]{2,1,0:T(8,128)(2,1)} %wa_ref.3) | copy-start | bytes 2359300
  117.1 25.2 %copy-start.5 = (f32[1424,512]{1,0:T(8,128)S(1)}, f32[1424,512]{1,0:T(8,128)}, u32[]{:S(2)}) copy-start(f32[1424,512]{1,0:T(8,128)} %get-tuple-element.58.gr_ref) | copy-start | bytes 8749060
  142.3 7.7 %copy-start.18 = (bf16[256,512]{1,0:T(8,128)(2,1)S(1)}, bf16[256,512]{1,0:T(8,128)(2,1)}, u32[]{:S(2)}) copy-start(bf16[256,512]{1,0:T(8,128)(2,1)} %get-tuple-element.67) | copy-start | bytes 786436
  142.3 10.3 %copy-start.14 = (bf16[256,512]{1,0:T(8,128)(2,1)S(1)}, bf16[256,512]{1,0:T(8,128)(2,1)}, u32[]{:S(2)}) copy-start(bf16[256,512]{1,0:T(8,128)(2,1)} %get-tuple-element.66) | copy-start | bytes 786436
  149.9 3.4 %collective-permute-start.5 = (bf16[3,512,256]{2,1,0:T(8,128)(2,1)S(1)}, bf16[3,512,256]{2,1,0:T(8,128)(2,1)S(1)}, u32[]{:S(2)}, u32[]{:S(2)}) collective-permute-start(bf16[3,512,256]{2,1,0:T(8,128)(2,1)S(1)} %get-tuple-element.61), channel_id=1, source_target_pairs={{0,1},{1,0},{2,3},{3,2},{4,5},{5,4},{6,7},{7,6},{8,9},{9,8},{10,11... | collective-permute-start | bytes 2359304 | tf_op jit(solution)/shard_map/ppermute | solution.py:471
  150.0 2.6 collective-permute-start.8
  152.6 1.9 copy-start.12
  154.4 1.3 copy-start.13
  157.1 0.8 copy-start.16
  157.1 0.9 copy-start.17
  157.1 0.9 copy-start.15
  158.1 1.2 collective-permute-start.7
  158.3 1.3 collective-permute-start.6
  313.0 4.3 %copy-start.11 = (bf16[512,1024]{1,0:T(8,128)(2,1)S(1)}, bf16[512,1024]{1,0:T(8,128)(2,1)}, u32[]{:S(2)}) copy-start(bf16[512,1024]{1,0:T(8,128)(2,1)} %get-tuple-element.74) | copy-start | bytes 3145732
  317.3 1.6 copy-start.10
Sparse Core Ops, SparseCore 0:
  157.2 155.7 all-reduce.2
